TPU v7x, 32 devices: a whole 2x2x4 slice. The times are simulated.
32 devices in a mesh: head: 2 (over x), blk: 16 (over z, y, core).
Axes of the slice: x: 2, y: 2, z: 4, core: 2. Of those that a mesh axis runs over, the one named last changes fastest.
Arguments:
- tokens: bfloat16 [4096, 768], P(('blk', 'head')), may hold values from -6 to 6
- cotangent: bfloat16 [4096, 768], P(('blk', 'head')), may hold values from -6 to 6
- prev_logits: float32 [4096, 12], P(('blk', 'head')), may hold values from -6 to 6
- routes: int32 [4096, 2], P(('blk', 'head')), may hold values from 0 to 11, all different within a row; in each aligned block of 128 rows (0 to 127, 128 to 255, ...) at most 24 rows name the same one
- lengths: int32 [2], replicated, may hold values from 512 to 2048, as said below
- w_qkv: bfloat16 [768, 2304], P(('head', 'blk')), may hold values from -0.21875 to 0.21875
- w_out: bfloat16 [768, 768], P(('head', 'blk')), may hold values from -3.5 to 3.5
- w_router: bfloat16 [768, 12], P(('head', 'blk')), may hold values from -0.109375 to 0.109375
- w_const: bfloat16 [768, 4], P(('head', 'blk')), may hold values from -0.21875 to 0.21875
- const_vec: bfloat16 [768, 2], P(('head', 'blk')), may hold values from -5 to 5
- norm_gains: bfloat16 [768, 2], P(('head', 'blk')), may hold values from 0.5 to 1.5
- gate_mix: float32 [12, 12], replicated, may hold values from -0.875 to 0.875
- expert_weights: bfloat16 [2048, 8, 3, 768], P('blk', 'head')
Outputs:
- output: bfloat16 [4096, 768], P(('blk', 'head'))
- aux_loss: float32 [], replicated
- d_tokens: bfloat16 [4096, 768], P(('blk', 'head'))
- g_qkv: float32 [768, 2304], P(('head', 'blk'))
- g_out: float32 [768, 768], P(('head', 'blk'))
- g_router: float32 [768, 12], P(('head', 'blk'))
- g_const: float32 [768, 4], P(('head', 'blk'))
- g_vector: float32 [768, 2], P(('head', 'blk'))
- g_gains: float32 [768, 2], P(('head', 'blk'))
- g_mix: float32 [12, 12], replicated
- g_experts: float32 [2048, 8, 3, 768], P('blk', 'head')
Inputs may be any that keep to these rules, and one draw needn't show every extreme that they name: `routes`: in each aligned block of 128 rows (the rows of one device), no expert is named by more than 24 rows; the two experts of a row differ. `lengths`: some slot's length is exactly 2048 in every draw.
All inputs are finite; a program needn't handle non-finite values.
Results may differ from a plain program's by a relative error of at most 0.015.
Values may be sent and summed in bfloat16 or wider, within the bound.
A program may use at most 256 MiB of HBM per device.

v0:
```python
from functools import partial
import functools
import math

import jax
import jax.numpy as jnp
import numpy as np
from jax import lax
from jax.experimental import pallas as pl
from jax.experimental.pallas import tpu as pltpu
from jax.sharding import PartitionSpec as P

HEADS = 12
MESH = pl.DeviceIdType.MESH
f32, bf16 = jnp.float32, jnp.bfloat16
NEG = -1e30
HD = 64
X, C, Y, Z = 1, 2, 4, 8
EARLY = (3, 2, 1)
Z_FIRST = (3, 2, 1)


def place(mask, h, b):
    hb = 1 - h if mask & X else h
    cb = b % 2
    yb = (b // 2) % 2
    zb = (b // 4) % 2
    cb = 1 - cb if mask & C else cb
    yb = 1 - yb if mask & Y else yb
    zb = 1 - zb if mask & Z else zb
    low = zb * 4 + yb * 2 + cb
    return hb, (b // 8) * 8 + low, low * 2 + hb


def head_of(h, b):
    quad = b % 4
    return h * 6 + ((b % 8) // 4) * 3 + quad - quad // 3


def home_of(head):
    h, i = head // 6, head % 6
    return ((i // 3) * 4 + i % 3) * 2 + h


def greet_all(h, b, n_blk):
    barrier = pltpu.get_barrier_semaphore()
    me = b * 2 + h
    total = 2 * n_blk

    def say(k, carry):
        other = (me + k) % total
        pl.semaphore_signal(barrier, inc=1, device_id=(other % 2, other // 2), device_id_type=MESH)
        return carry

    lax.fori_loop(1, total, say, 0)
    return lambda: pl.semaphore_wait(barrier, total - 1)


def turned(qk, cos, sin):
    lane = lax.broadcasted_iota(jnp.int32, qk.shape, 1)
    swapped = jnp.where(lane % 64 < 32, pltpu.roll(qk, 96, 1), pltpu.roll(qk, 32, 1))
    return qk * cos + swapped * sin


def rotary_tables(rows):
    freq = np.exp(np.arange(32, dtype=np.float32) * np.float32(-2.0 * math.log(10000.0) / 64)).astype(np.float32)
    ang = (np.arange(rows, dtype=np.float32)[:, None] * freq[None, :]).astype(np.float32).astype(np.float64)
    cos, sin = np.cos(ang), np.sin(ang)
    return (
        np.concatenate([cos, cos, cos, cos], 1).astype(np.float32),
        np.concatenate([-sin, sin, -sin, sin], 1).astype(np.float32),
    )


class RowGather:
    def __init__(self, buf, sems, h, b, straight=False):
        self.buf, self.h, self.b, self.straight = buf, h, b, straight
        self.parts = range(buf.shape[1])
        self.zs, self.ys, self.cs, self.zr, self.yr, self.cr = sems
        self.z, self.y, self.c = b // 4, (b // 2) % 2, b % 2

    def nth(self, k):
        return nearest(self.z, k)

    def at(self, z, y, c, p):
        return self.buf.at[z * 4 + y * 2 + c, p]

    def copy(self, where, send, recv, device):
        return pltpu.make_async_remote_copy(
            src_ref=where, dst_ref=where, send_sem=send, recv_sem=recv, device_id=device, device_id_type=MESH)

    def along_z(self, k, step, p):
        zz = self.nth(k)
        return self.copy(self.at(zz, self.y, self.c, p), self.zs.at[(step + 1) // 2, k, p], self.zr.at[zz, p],
                         (self.h, self.b + 4 * step))

    def to_z(self, k, p):
        return self.copy(self.at(self.z, self.y, self.c, p), self.zs.at[0, k, p], self.zr.at[self.z, p],
                         (self.h, self.nth(k) * 4 + self.b % 4))

    def over_y(self, k, p):
        zz = self.nth(k)
        return self.copy(self.at(zz, self.y, self.c, p), self.ys.at[k, p], self.yr.at[zz, p],
                         (self.h, self.b + 2 - 4 * self.y))

    def over_core(self, k, far, p):
        zz = self.nth(k)
        yy = 1 - self.y if far else self.y
        return self.copy(self.at(zz, yy, self.c, p), self.cs.at[far, k, p], self.cr.at[far, zz, p],
                         (self.h, self.b + 1 - 2 * self.c))

    def own_z(self, act):
        for p in self.parts:
            if self.straight:
                for k in range(1, 4):
                    act(self.to_z(k, p))
            else:
                for step in (1, -1):
                    @pl.when((self.z + step >= 0) & (self.z + step <= 3))
                    def _(step=step, p=p):
                        act(self.along_z(0, step, p))

    def relay(self, k, p, act):
        if self.straight:
            return
        zz = self.nth(k)

        @pl.when((zz < self.z) & (self.z < 3))
        def _():
            act(self.along_z(k, 1, p))

        @pl.when((zz > self.z) & (self.z > 0))
        def _():
            act(self.along_z(k, -1, p))

    def start(self):
        self.own_z(lambda c: c.start())
        for p in self.parts:
            self.over_y(0, p).start()
        for p in self.parts:
            self.over_core(0, 0, p).start()

    def arrived(self, where, sem):
        self.copy(where, self.zs.at[0, 0, 0], sem, (self.h, self.b)).wait_recv()

    def got_z(self, k):
        zz = self.nth(k)
        for p in self.parts:
            self.arrived(self.at(zz, self.y, self.c, p), self.zr.at[zz, p])
            self.relay(k, p, lambda c: c.start())
            self.over_y(k, p).start()
            self.over_core(k, 0, p).start()

    def got_y(self, k):
        zz = self.nth(k)
        for p in self.parts:
            self.arrived(self.at(zz, 1 - self.y, self.c, p), self.yr.at[zz, p])
            self.over_core(k, 1, p).start()

    def got_core(self, k):
        zz = self.nth(k)
        for far in range(2):
            yy = 1 - self.y if far else self.y
            for p in self.parts:
                self.arrived(self.at(zz, yy, 1 - self.c, p), self.cr.at[far, zz, p])

    def finish(self):
        self.own_z(lambda c: c.wait_send())
        for p in self.parts:
            for k in range(4):
                if k:
                    self.relay(k, p, lambda c: c.wait_send())
                self.over_y(k, p).wait_send()
                self.over_core(k, 0, p).wait_send()
                self.over_core(k, 1, p).wait_send()


def nearest(z, k):
    near = z - (z // 2) * (2 * z - 3)
    low = k + (1 - 2 * k) * near if k < 2 else k
    return low + (z // 2) * (3 - 2 * low)


def gather_sems(parts):
    DMA = pltpu.SemaphoreType.DMA
    return [DMA((2, 4, parts)), DMA((4, parts)), DMA((2, 4, parts)), DMA((4, parts)), DMA((4, parts)), DMA((2, 4, parts))]


def fold(rows):
    half = rows.shape[1] // 2
    low = jnp.concatenate([rows[16:24, :half], rows[16:24, half:]], axis=0)
    return jnp.concatenate([rows[0:16], low], axis=1).astype(bf16)


def routing_table(routes, live):
    lane = lax.broadcasted_iota(jnp.int32, (128, 128), 1)
    row = lax.broadcasted_iota(jnp.int32, (128, 128), 0)
    expert = lane.astype(f32)
    named = jnp.where((routes[:, 0:1] == expert) | (routes[:, 1:2] == expert), live, 0.0)
    before = jnp.where(lane < row, 1.0, 0.0).astype(bf16)
    rank = jnp.dot(before, named.astype(bf16), preferred_element_type=f32)
    return named, named * (rank + 1.0)


def expert_lanes(h):
    e = lax.broadcasted_iota(jnp.int32, (128, 256), 0)
    s = lax.broadcasted_iota(jnp.int32, (128, 256), 1)
    return jnp.where((s < 192) & (e == 4 * h + s // 48), 1.0, 0.0)


def slot_table(ranks, h, source_h):
    spread = jnp.dot(ranks.astype(bf16), expert_lanes(h).astype(bf16), preferred_element_type=f32)
    s = lax.broadcasted_iota(jnp.int32, (128, 256), 1)
    place_in = s % 48 - 24 * source_h
    inside = (place_in >= 0) & (place_in < 24) & (s < 192)
    return jnp.where(inside & (spread == (place_in + 1).astype(f32)), 1.0, 0.0)


def live_column(h, b, length):
    row = lax.broadcasted_iota(jnp.int32, (128, 1), 0) + ((b % 8) * 2 + h) * 128
    return jnp.where(row < length, 1.0, 0.0)


def forward_kernel(
    n_blk, all_here, lengths, tok, cot, routes, w_in, small, wo_in, cos_hbm, sin_hbm, relay_w,
    norm_hbm, q_hbm, k_hbm, v_hbm, o_hbm, att_out, smt_out, cnt_out, sm_out, wo_out, pt_out, cot_rows,
    xg, pieces, got, w_f, w_b, cos, sin, norm, q, k, v, o, sendbuf, att_in, rank_own, rank_far, cot_far, wo_all,
    ag_send, ag_recv, pc_send, pc_recv, at_send, at_recv, loc, x_send, x_recv, *gathers,
):
    h, b = lax.axis_index("head"), lax.axis_index("blk")
    me = b * 2 + h
    total = 2 * n_blk
    _, _, rank = place(0, h, b)
    cos_in = pltpu.make_async_copy(cos_hbm, cos, loc.at[9])
    sin_in = pltpu.make_async_copy(sin_hbm, sin, loc.at[10])
    cos_in.start()
    sin_in.start()
    for p in range(3):
        xg[p, rank] = tok[:, 256 * p : 256 * p + 256]
    all_here()

    def block_copy(p, m, d, slot):
        _, _, r = place(m, h, b)
        ph, pb, _ = place(d, h, b)
        return pltpu.make_async_remote_copy(
            src_ref=xg.at[p, r], dst_ref=xg.at[p, r],
            send_sem=ag_send.at[p, slot], recv_sem=ag_recv.at[p, m ^ d],
            device_id=(ph, pb), device_id_type=MESH,
        )

    def arrival(p, m):
        _, _, r = place(m, h, b)
        return pltpu.make_async_remote_copy(
            src_ref=xg.at[p, r], dst_ref=xg.at[p, r],
            send_sem=ag_send.at[p, 0], recv_sem=ag_recv.at[p, m],
            device_id=(h, b), device_id_type=MESH,
        )

    sends = []
    counts = [0, 0, 0]

    def send(p, m, d):
        copy = block_copy(p, m, d, counts[p])
        counts[p] += 1
        copy.start()
        sends.append(copy)

    dims = [X, Y, Z]
    orders = [dims[p:] + dims[:p] for p in range(3)]
    for t in range(3):
        for p in range(3):
            send(p, 0, orders[p][t])
    for p in range(3):
        send(p, 0, C)

    length = lengths[b // 8]
    named, ranks = routing_table(routes[...], live_column(h, b, length))
    rank_own[...] = ranks.astype(bf16)
    wo_all[b, 0, h] = fold(wo_in[...].astype(f32))

    w24 = w_in[...].astype(f32)
    count = pltpu.roll(jnp.sum(named, axis=0, keepdims=True), 20, 1)[:, 0:64]
    small = small[...] + jnp.where(lax.broadcasted_iota(jnp.int32, (24, 64), 0) == 0, count, 0.0)
    for j in range(12):
        cat = jnp.concatenate(
            [w24[:, 64 * j : 64 * j + 64], w24[:, 768 + 64 * j : 832 + 64 * j],
             w24[:, 1536 + 64 * j : 1600 + 64 * j], small], axis=1)
        pieces[j] = fold(cat)

    def piece_copy(kk):
        other = (me + kk) % total
        oh, ob = other % 2, other // 2
        return pltpu.make_async_remote_copy(
            src_ref=pieces.at[head_of(oh, ob)], dst_ref=got.at[me],
            send_sem=pc_send.at[kk], recv_sem=pc_recv.at[me],
            device_id=(oh, ob), device_id_type=MESH,
        )

    def send_piece(kk, carry):
        piece_copy(kk).start()
        return carry

    lax.fori_loop(1, total, send_piece, 0)
    got[me] = pieces[head_of(h, b)]

    relay_w(0)
    for p in range(3):
        d0, d1, d2 = orders[p]
        arrival(p, d0).wait_recv()
        for d in (d1, d2, C):
            send(p, d0, d)
    relay_w(1)
    for p in range(3):
        d0, d1, d2 = orders[p]
        for m in (d1, d0 ^ d1):
            arrival(p, m).wait_recv()
            for d in (d2, C):
                send(p, m, d)
    swaps = [
        pltpu.make_async_remote_copy(
            src_ref=src, dst_ref=dst, send_sem=x_send.at[n], recv_sem=x_recv.at[n],
            device_id=(1 - h, b), device_id_type=MESH)
        for n, (src, dst) in enumerate([(wo_all.at[b, 0, h], wo_all.at[b, 0, h]), (rank_own, rank_far), (cot, cot_far)])
    ]
    for c in swaps:
        c.start()
    relay_w(2)
    for p in range(3):
        d0, d1, d2 = orders[p]
        for m in (d2, d0 ^ d2, d1 ^ d2, d0 ^ d1 ^ d2):
            arrival(p, m).wait_recv()
            send(p, m, C)

    def take_piece(kk, carry):
        src = (me + kk) % total
        pltpu.make_async_remote_copy(
            src_ref=pieces.at[0], dst_ref=got.at[src],
            send_sem=pc_send.at[0], recv_sem=pc_recv.at[src],
            device_id=(h, b), device_id_type=MESH,
        ).wait_recv()
        return carry

    lax.fori_loop(1, total, take_piece, 0)

    for src in range(2 * n_blk):
        row = 24 * ((src % 2) * n_blk + src // 2)
        w_f[row : row + 16, :] = got[src, :, 0:256].astype(f32)
        low = got[src, :, 256:384].astype(f32)
        w_f[row + 16 : row + 24, 0:128] = low[0:8]
        w_f[row + 16 : row + 24, 128:256] = low[8:16]
    w_b[...] = w_f[...].astype(bf16)
    sm = pltpu.roll(w_f[:, 128:256], 64, 1)
    lane = lax.broadcasted_iota(jnp.int32, (768, 128), 1)
    cnt = jnp.sum(jnp.where((lane >= 20) & (lane < 32), sm, 0.0), axis=0, keepdims=True)
    cnt_out[...] = jnp.broadcast_to(pltpu.roll(cnt, 108, 1), (8, 128))
    sm = jnp.where(lane < 20, sm, 0.0)
    sm_out[...] = sm.astype(bf16)
    smt = jnp.transpose(sm)
    smt_out[...] = smt[0:32, :]
    gain = smt[16:17, :]

    pltpu.make_async_remote_copy(
        src_ref=wo_all.at[b, 0, h], dst_ref=wo_all.at[b, 0, 1 - h], send_sem=x_send.at[0], recv_sem=x_recv.at[0],
        device_id=(h, b), device_id_type=MESH).wait_recv()
    wo_gather = RowGather(wo_all, gathers[0:6], h, b, straight=True)
    wo_gather.start()
    swaps[1].wait_recv()
    swaps[2].wait_recv()
    pt = [slot_table(ranks, h, h).astype(bf16), slot_table(rank_far[...].astype(f32), h, 1 - h).astype(bf16)]
    pt_out[0] = pt[0]
    pt_out[1] = pt[1]
    picked = sum(
        lax.dot_general(t[:, 0:192], c[...], (((0,), (0,)), ((), ())), preferred_element_type=f32)
        for t, c in zip(pt, (cot, cot_far))).astype(bf16)
    cot_rows[b, 0] = picked[0:96]
    cot_rows[b, 1] = picked[96:192]
    cot_gather = RowGather(cot_rows, gathers[6:12], h, b, straight=True)
    cot_gather.start()

    cos_in.wait()
    sin_in.wait()

    def one_block(r, carry):
        x = [xg[p, r].astype(f32) for p in range(3)]
        mean = sum(jnp.sum(t * t, axis=1, keepdims=True) for t in x) * (1.0 / 768)
        scale = lax.rsqrt(mean + 1e-6)
        rows = pl.ds(pl.multiple_of(r * 128, 128), 128)
        acc = jnp.zeros((128, 256), f32)
        for p in range(3):
            n = (x[p] * scale * gain[:, 256 * p : 256 * p + 256]).astype(bf16)
            norm[rows, 256 * p : 256 * p + 256] = n
            acc = acc + jnp.dot(n, w_b[256 * p : 256 * p + 256, :], preferred_element_type=f32)
        qk = turned(acc[:, 0:128], cos[rows, :], sin[rows, :])
        q[rows, :] = (qk[:, 0:64] * 0.125).astype(bf16)
        k[rows, :] = qk[:, 64:128].astype(bf16)
        lane = lax.broadcasted_iota(jnp.int32, (128, 128), 1)
        v[rows, :] = jnp.where(lane < 64, acc[:, 128:256], jnp.where(lane == 64, 1.0, 0.0)).astype(bf16)
        return carry

    def of_core(core):
        return lambda i, carry: one_block((i // 4) * 8 + ((i // 2) % 2) * 4 + core * 2 + i % 2, carry)

    lax.fori_loop(0, 8, of_core(b % 2), 0)
    for p in range(3):
        for m in (C, C ^ X, C ^ Y, C ^ Z, C ^ X ^ Y, C ^ X ^ Z, C ^ Y ^ Z, C ^ X ^ Y ^ Z):
            arrival(p, m).wait_recv()
    lax.fori_loop(0, 8, of_core(1 - b % 2), 0)
    stores = [
        pltpu.make_async_copy(norm, norm_hbm, loc.at[4]),
        pltpu.make_async_copy(q, q_hbm, loc.at[5]),
        pltpu.make_async_copy(k, k_hbm, loc.at[6]),
        pltpu.make_async_copy(v, v_hbm, loc.at[7]),
    ]
    for s in stores:
        s.start()

    head = head_of(h, b)
    working = (b % 4) != 3
    base = (b // 8) * 8

    w, c = wo_gather, cot_gather
    between = {
        0: [lambda: w.got_z(1), lambda: w.got_y(0)],
        1: [lambda: w.got_z(2), lambda: w.got_z(3)],
        2: [lambda: w.got_y(1)],
        3: [lambda: w.got_y(2), lambda: c.got_z(1)],
        4: [lambda: w.got_y(3)],
        5: [lambda: w.got_core(0), lambda: w.got_core(1), lambda: c.got_y(0)],
        6: [lambda: w.got_core(2), lambda: w.got_core(3)],
        7: [],
    }

    def out_copy(r):
        return pltpu.make_async_remote_copy(
            src_ref=sendbuf.at[r], dst_ref=att_in.at[head],
            send_sem=at_send.at[r], recv_sem=at_recv.at[head],
            device_id=(r % 2, base + r // 2), device_id_type=MESH,
        )

    for i in range(8):
        width = 256 * (i + 1)
        s = lax.dot_general(q[256 * i : width, :], k[0:width, :], (((1,), (1,)), ((), ())), preferred_element_type=f32)
        key = lax.broadcasted_iota(jnp.int32, (1, width), 1)
        s = s + jnp.where(key < length, 0.0, NEG)
        rowi = lax.broadcasted_iota(jnp.int32, (256, 256), 0)
        coli = lax.broadcasted_iota(jnp.int32, (256, 256), 1)
        last = jnp.where(coli <= rowi, s[:, width - 256 :], NEG)
        s = last if i == 0 else jnp.concatenate([s[:, : width - 256], last], axis=1)
        m = jnp.max(s, axis=1, keepdims=True)
        e = jnp.exp(s - m).astype(bf16)
        ov = jnp.dot(e, v[0:width, :], preferred_element_type=f32)
        l = ov[:, 64:65]
        lane = lax.broadcasted_iota(jnp.int32, (256, 128), 1)
        ov = jnp.where(lane < 64, ov / l, m + jnp.log(l))
        o[256 * i : width, :] = ov
        oh = ov[:, 0:64]
        for half in range(2):
            r = 2 * i + half
            packed = jnp.concatenate([oh[128 * half : 128 * half + 64], oh[128 * half + 64 : 128 * half + 128]], axis=1)
            sendbuf[r] = packed.astype(bf16)

            @pl.when(working & (r != rank))
            def _(r=r):
                out_copy(r).start()
        for act in between[i]:
            act()

    o_store = pltpu.make_async_copy(o, o_hbm, loc.at[8])
    o_store.start()

    def unfolded(blk, hh):
        t = wo_all[blk, 0, hh].astype(f32)
        return jnp.concatenate(
            [t[:, 0:768], jnp.concatenate([t[0:8, 768:1152], t[8:16, 768:1152]], axis=1)], axis=0)

    for hh in range(2):
        for blk in range(0, 16, 2):
            row = 24 * (hh * 16 + blk)
            wo_out[row : row + 48, :] = jnp.concatenate([unfolded(blk, hh), unfolded(blk + 1, hh)], axis=0).astype(bf16)

    @pl.when(working)
    def _():
        att_in[head] = sendbuf[rank]

    for j in range(12):
        @pl.when(rank != home_of(j))
        def _(j=j):
            pltpu.make_async_remote_copy(
                src_ref=sendbuf.at[0], dst_ref=att_in.at[j],
                send_sem=at_send.at[0], recv_sem=at_recv.at[j],
                device_id=(h, b), device_id_type=MESH,
            ).wait_recv()

    for j in range(0, 12, 2):
        one, two = att_in[j].astype(f32), att_in[j + 1].astype(f32)
        att_out[0:64, 64 * j : 64 * j + 128] = jnp.concatenate([one[:, 0:64], two[:, 0:64]], axis=1).astype(bf16)
        att_out[64:128, 64 * j : 64 * j + 128] = jnp.concatenate([one[:, 64:128], two[:, 64:128]], axis=1).astype(bf16)

    def finish():
        for copy in sends:
            copy.wait_send()
        for c in swaps:
            c.wait_send()
        wo_gather.finish()
        cot_gather.finish()

        def sent_piece(kk, carry):
            piece_copy(kk).wait_send()
            return carry

        lax.fori_loop(1, total, sent_piece, 0)
        for r in range(16):
            @pl.when(working & (r != rank))
            def _(r=r):
                out_copy(r).wait_send()
        for s in stores:
            s.wait()
        o_store.wait()

    return cot_gather, finish


def split(x):
    high = x.astype(bf16)
    return high, (x - high.astype(f32)).astype(bf16)


def exact_dot(x, y, dims):
    high, low = split(x)
    return lax.dot_general(high, y, (dims, ((), ())), preferred_element_type=f32) + lax.dot_general(
        low, y, (dims, ((), ())), preferred_element_type=f32)


def softmax_back(p, d):
    return p * (d - jnp.sum(p * d, axis=1, keepdims=True))


def lane_of(column, n):
    lane = lax.broadcasted_iota(jnp.int32, (128, 128), 1)
    return jnp.where(lane == n, column, 0.0)


class RowScatter:
    def __init__(self, part, from_core, from_y, from_z, sems, h, b):
        self.part, self.from_core, self.from_y, self.from_z = part, from_core, from_y, from_z
        self.h, self.b = h, b
        self.cs, self.cr, self.ys, self.yr, self.zs, self.zr = sems
        self.parts = range(part.shape[1])
        self.order = [(k, p) for k in (3, 2, 1, 0) for p in self.parts]
        self.z, self.y, self.c = b // 4, (b // 2) % 2, b % 2

    def nth(self, k):
        return nearest(self.z, k)

    def blk(self, k, far_y, far_c):
        y = 1 - self.y if far_y else self.y
        c = 1 - self.c if far_c else self.c
        return self.nth(k) * 4 + y * 2 + c

    def remote(self, src, dst, send, recv, device):
        return pltpu.make_async_remote_copy(
            src_ref=src, dst_ref=dst, send_sem=send, recv_sem=recv, device_id=device, device_id_type=MESH)

    def core(self, k, far, p):
        return self.remote(self.part.at[self.blk(k, far, 1), p], self.from_core.at[k, far, p], self.cs.at[k, far, p],
                           self.cr.at[k, far, p], (self.h, self.b + 1 - 2 * self.c))

    def over_y(self, k, p):
        return self.remote(self.part.at[self.blk(k, 1, 0), p], self.from_y.at[k, p], self.ys.at[k, p], self.yr.at[k, p],
                           (self.h, self.b + 2 - 4 * self.y))

    def to_z(self, k, p):
        return self.remote(self.part.at[self.blk(k, 0, 0), p], self.from_z.at[self.z, p], self.zs.at[k, p],
                           self.zr.at[self.z, p], (self.h, self.nth(k) * 4 + self.b % 4))

    def join_y(self, k, p):
        self.core(k, 0, p).wait_recv()
        self.over_y(k, p).wait_recv()
        self.add(self.blk(k, 0, 0), p, self.from_core.at[k, 0, p], self.from_y.at[k, p])

    def add(self, blk, p, *others):
        total = self.part[blk, p].astype(f32)
        for other in others:
            total = total + other[...].astype(f32)
        self.part[blk, p] = total.astype(bf16)

    def send_core(self, k, p):
        self.core(k, 1, p).start()
        self.core(k, 0, p).start()

    def send_y(self, k, p):
        self.core(k, 1, p).wait_recv()
        self.add(self.blk(k, 1, 0), p, self.from_core.at[k, 1, p])
        self.over_y(k, p).start()

    def send_z(self, k, p):
        self.join_y(k, p)
        if k:
            self.to_z(k, p).start()

    def total(self, p):
        total = self.part[self.b, p].astype(f32)
        for k in range(1, 4):
            here = self.from_z.at[self.nth(k), p]
            self.remote(here, here, self.zs.at[0, 0], self.zr.at[self.nth(k), p], (self.h, self.b)).wait_recv()
            total = total + here[...].astype(f32)
        return total

    def finish(self, near=range(4), far=range(1, 4)):
        for p in self.parts:
            for k in near:
                self.core(k, 0, p).wait_send()
                self.core(k, 1, p).wait_send()
                self.over_y(k, p).wait_send()
            for k in far:
                self.to_z(k, p).wait_send()


def scatter_scratch(parts, rows, cols):
    DMA = pltpu.SemaphoreType.DMA
    V = pltpu.VMEM
    return [
        V((4, 2, parts, rows, cols), bf16), V((4, parts, rows, cols), bf16), V((4, parts, rows, cols), bf16),
        DMA((4, 2, parts)), DMA((4, 2, parts)), DMA((4, parts)), DMA((4, parts)), DMA((4, parts)), DMA((4, parts)),
    ]


def expert_kernel(
    n_blk, cg, lengths, att, tok, cot, prev, mix, routes, wout, sm, smt, cnt, pt, w, cot_all,
    part_hbm, g_hbm, local_out, res_out, ag_out, gs_out, misc_out, pg_out,
    x_all, cc, dgu, hid, inp, outp, gbuf, gates_in, vs_out, vs_in, n_own, n_far, g_own, g_far,
    d_out, d_in, dv_out, dv_in, ga_send, ga_recv, vs_send, vs_recv, x_send, x_recv, loc, *rest,
):
    gsems, (from_core, from_y, from_z), ssems, (out_core, out_y), osems = rest[0:6], rest[6:9], rest[9:15], rest[15:17], rest[17:21]
    h, b = lax.axis_index("head"), lax.axis_index("blk")
    length = lengths[b // 8]
    live_total = (lengths[0] + lengths[1]).astype(f32)
    live = live_column(h, b, length)
    lane = lax.broadcasted_iota(jnp.int32, (128, 128), 1)

    res = tok[...].astype(f32) + jnp.dot(att[...], wout[...], preferred_element_type=f32)
    scale = lax.rsqrt(jnp.sum(res * res, axis=1, keepdims=True) * (1.0 / 768) + 1e-6)
    xh = res * scale
    n2 = (xh * smt[17:18, :]).astype(bf16)
    small = sm[...]
    logits = jnp.dot(n2, small, preferred_element_type=f32)
    router = logits + jnp.dot(prev[...], mix[...], preferred_element_type=f32, precision=lax.Precision.HIGHEST)
    router = jnp.where(lane < 12, router, NEG)
    prob = jnp.exp(router - jnp.max(router, axis=1, keepdims=True))
    prob = prob / jnp.sum(prob, axis=1, keepdims=True)
    expert = lane.astype(f32)
    named = jnp.where((routes[:, 0:1] == expert) | (routes[:, 1:2] == expert), 1.0, 0.0)
    gates = prob * named
    n_own[...] = n2
    g_own[...] = gates
    swaps = [
        pltpu.make_async_remote_copy(
            src_ref=src, dst_ref=dst, send_sem=x_send.at[n], recv_sem=x_recv.at[n],
            device_id=(1 - h, b), device_id_type=MESH)
        for n, (src, dst) in enumerate([(n_own, n_far), (g_own, g_far), (d_out, d_in), (dv_out, dv_in)])
    ]
    swaps[0].start()
    swaps[1].start()
    cg.got_z(2)
    cg.got_y(1)
    p_own, p_far = pt[0, :, 0:192], pt[1, :, 0:192]
    rows = ((0,), (0,))
    mine = lax.dot_general(p_own, n2, (rows, ((), ())), preferred_element_type=f32)
    spread = expert_lanes(h).astype(bf16)
    pg_own = pt[0].astype(f32) * exact_dot(gates, spread, ((1,), (0,)))
    pg_out[0] = pg_own
    swaps[0].wait_recv()
    picked = (mine + lax.dot_general(p_far, n_far[...], (rows, ((), ())), preferred_element_type=f32)).astype(bf16)
    x_all[b, 0] = picked[0:96]
    x_all[b, 1] = picked[96:192]
    g = RowGather(x_all, gsems, h, b)
    g.start()
    cg.got_z(3)
    cg.got_y(2)
    cg.got_y(3)
    swaps[1].wait_recv()
    pg_far = pt[1].astype(f32) * exact_dot(g_far[...], spread, ((1,), (0,)))
    pg_out[1] = pg_far
    gates_in[b] = jnp.broadcast_to(jnp.sum(pg_own + pg_far, axis=0, keepdims=True), (8, 256))

    def gate_copy(k):
        return pltpu.make_async_remote_copy(
            src_ref=gates_in.at[b], dst_ref=gates_in.at[b], send_sem=ga_send.at[k], recv_sem=ga_recv.at[b],
            device_id=(h, (b + k) % n_blk), device_id_type=MESH)

    def vs_copy(k):
        to = (b + k) % n_blk
        return pltpu.make_async_remote_copy(
            src_ref=vs_out.at[to], dst_ref=vs_in.at[b], send_sem=vs_send.at[k], recv_sem=vs_recv.at[b],
            device_id=(h, to), device_id_type=MESH)

    def each(act):
        def body(k, carry):
            act(k)
            return carry

        lax.fori_loop(1, n_blk, body, 0)

    each(lambda k: gate_copy(k).start())

    def group(ref, k, p, ee):
        return ref[pl.ds(4 * g.nth(k), 4), p, 48 * ee : 48 * ee + 48, :]

    def put(ref, k, p, ee, value):
        ref[pl.ds(4 * g.nth(k), 4), p, 48 * ee : 48 * ee + 48, :] = value.reshape(4, 48, value.shape[1]).astype(ref.dtype)

    cols = ((1,), (1,))

    def cot_task(k):
        for e in range(4):
            rows_c = group(cot_all, k, e // 2, e % 2).reshape(192, 768)
            put(cc, k, e // 2, e % 2, lax.dot_general(rows_c, w[3 * e + 2], (cols, ((), ())), preferred_element_type=f32))

    def up_task(k):
        for e in range(4):
            p, ee = e // 2, e % 2
            x = group(x_all, k, p, ee).reshape(192, 768)
            both = lax.dot_general(x, w[3 * e : 3 * e + 2].reshape(256, 768), (cols, ((), ())), preferred_element_type=f32)
            gate, up = both[:, 0:128], both[:, 128:256]
            sig = 1.0 / (1.0 + jnp.exp(-gate))
            silu = gate * sig
            hidden = silu * up
            c = group(cc, k, p, ee).reshape(192, 128)
            put(hid, k, p, ee, hidden)
            put(cc, k, p, ee, hidden * c)
            dg = c * up * (sig * (1.0 + gate * (1.0 - sig)))
            put(dgu, k, p, ee, jnp.concatenate([dg, c * silu], axis=1))

    two = jnp.where(lane % 2 == 0, pltpu.roll(logits, 127, 1), pltpu.roll(logits, 1, 1))
    top = jnp.maximum(logits, two)
    c_mix = jnp.exp(logits - top) / (jnp.exp(logits - top) + jnp.exp(two - top))
    share = gates * live
    n2f = n2.astype(f32)
    alpha = share[:, 9:10] + share[:, 10:11] * c_mix[:, 12:13] + share[:, 11:12] * c_mix[:, 14:15]
    beta = [share[:, 10:11] * c_mix[:, 13:14], share[:, 11:12] * c_mix[:, 15:16]]
    local_out[...] = live * (res + alpha * n2f + beta[0] * smt[18:19, :] + beta[1] * smt[19:20, :])
    og = live * cot[...].astype(f32)
    og_low = og.astype(bf16)

    g.got_z(1)
    cg.got_core(0)
    cot_task(0)
    g.got_z(2)
    g.got_y(0)
    cg.got_core(1)
    cot_task(1)
    g.got_z(3)
    g.got_y(1)
    cg.got_core(2)
    cot_task(2)
    cg.got_core(3)
    cot_task(3)
    g.got_core(0)
    up_task(0)
    g.got_y(2)
    g.got_core(1)
    up_task(1)
    g.got_y(3)
    g.got_core(2)
    up_task(2)
    g.got_core(3)
    up_task(3)

    s = RowScatter(inp, from_core, from_y, from_z, ssems, h, b)
    order = s.order
    for n, (k, p) in enumerate(order):
        for ee in range(2):
            e = 2 * p + ee
            d = group(dgu, k, p, ee).reshape(192, 256)
            put(inp, k, p, ee, jnp.dot(d, w[3 * e : 3 * e + 2].reshape(256, 768), preferred_element_type=f32))
        s.send_core(k, p)
        if n:
            s.send_y(*order[n - 1])
    s.send_y(*order[7])

    ones = jnp.ones((8, 128), f32)

    def one_blk(j, carry):
        for p in range(2):
            vs_out[j, :, 128 * p : 128 * p + 96] = lax.dot_general(
                ones, cc[j, p], (cols, ((), ())), preferred_element_type=f32, precision=lax.Precision.HIGHEST)
        return carry

    lax.fori_loop(0, n_blk, one_blk, 0)
    each(lambda k: vs_copy(k).start())
    vs_in[b] = vs_out[b]
    each(lambda k: pltpu.make_async_remote_copy(
        src_ref=gates_in.at[b], dst_ref=gates_in.at[(b + k) % n_blk], send_sem=ga_send.at[0],
        recv_sem=ga_recv.at[(b + k) % n_blk], device_id=(h, b), device_id_type=MESH).wait_recv())
    gate_cols = jnp.transpose(gates_in[:, 0, :])

    def scaled(ref, p, ee):
        e = 2 * p + ee
        t = ref[:, p, 48 * ee : 48 * ee + 48, :].astype(f32)
        col = jnp.concatenate([gate_cols[48 * e : 48 * e + 48, j : j + 1] for j in range(n_blk)], axis=0)
        return (t.reshape(48 * n_blk, t.shape[2]) * col).astype(bf16)

    def store_g(e, act):
        for kind in range(3):
            act(pltpu.make_async_copy(gbuf.at[kind], g_hbm.at[:, kind, e, :], loc.at[kind]))

    def weight_task(e):
        p, ee = e // 2, e % 2
        x = x_all[:, p, 48 * ee : 48 * ee + 48, :].reshape(48 * n_blk, 768)
        c = cot_all[:, p, 48 * ee : 48 * ee + 48, :].reshape(48 * n_blk, 768)
        if e:
            store_g(e - 1, lambda c: c.wait())
        gbuf[0:2] = lax.dot_general(
            scaled(dgu, p, ee), x, (rows, ((), ())), preferred_element_type=f32).reshape(2, 128, 768)
        gbuf[2] = lax.dot_general(scaled(hid, p, ee), c, (rows, ((), ())), preferred_element_type=f32)
        store_g(e, lambda c: c.start())

    def out_task(k):
        for e in range(4):
            d = group(hid, k, e // 2, e % 2).reshape(192, 128)
            put(outp, k, e // 2, e % 2, jnp.dot(d, w[3 * e + 2], preferred_element_type=f32))

    outs = RowScatter(outp, out_core, out_y, None, (*osems, None, None), h, b)
    early = [(k, p) for k in EARLY for p in range(2)]

    def send_early():
        for n in early:
            outs.send_core(*n)
        for n in early:
            outs.send_y(*n)

    tasks = [[lambda: out_task(3), lambda: out_task(2)], [lambda: out_task(1), lambda: out_task(0)], [send_early],
             [lambda: weight_task(0)], [lambda: weight_task(1)], [lambda: weight_task(2)], [lambda: weight_task(3)], []]
    def sum_step(n):
        for act in tasks[n]:
            act()
        s.send_z(*order[n])

    def part_store(k, whole):
        zz = g.nth(k)
        at = pl.ds(4 * zz, 4) if whole else pl.ds(outs.blk(k, 0, 0), 1)
        return pltpu.make_async_copy(outp.at[at], part_hbm.at[at], loc.at[3 + k])

    for n in range(6):
        sum_step(n)
    for k in range(4):
        if k not in EARLY:
            part_store(k, True).start()

    each(lambda k: pltpu.make_async_remote_copy(
        src_ref=vs_in.at[b], dst_ref=vs_in.at[(b + k) % n_blk], send_sem=vs_send.at[0],
        recv_sem=vs_recv.at[(b + k) % n_blk], device_id=(h, b), device_id_type=MESH).wait_recv())
    vsum = jnp.sum(vs_in[:, 0, :], axis=0, keepdims=True)
    vrow = jnp.concatenate([vsum[:, 0:96], vsum[:, 128:224]], axis=1)
    spread = spread[:, 0:192]
    dv_out[...] = exact_dot(p_far.astype(f32) * vrow, spread, cols)
    swaps[3].start()
    dv_own = exact_dot(p_own.astype(f32) * vrow, spread, cols)
    u = jnp.sum(og * n2f, axis=1, keepdims=True)
    wj = jnp.dot(og_low, small, preferred_element_type=f32)
    w0, w1 = wj[:, 18:19], wj[:, 19:20]
    c = [c_mix[:, n : n + 1] for n in (12, 13, 14, 15)]
    dgate = lane_of(u, 9) + lane_of(c[0] * u + c[1] * w0, 10) + lane_of(c[2] * u + c[3] * w1, 11)
    dmix = lane_of(u, 12) + lane_of(w0, 13) + lane_of(u, 14) + lane_of(w1, 15)
    dmix = dmix * jnp.where(lane < 14, gates[:, 10:11], gates[:, 11:12])
    both = c_mix * dmix
    dmix = c_mix * (dmix - both - jnp.where(lane % 2 == 0, pltpu.roll(both, 127, 1), pltpu.roll(both, 1, 1)))
    dmix = jnp.where((lane >= 12) & (lane < 16), dmix, 0.0)
    aux = (0.01 * 12.0 / live_total) * (cnt[0:1, :] / (2.0 * live_total)) * live
    sum_step(6)
    swaps[3].wait_recv()
    dprob = named * (dgate + dv_own + dv_in[...]) + aux
    dlog = softmax_back(prob, dprob) + dmix
    dn_near = og * alpha + exact_dot(dlog, jnp.where(
        lax.broadcasted_iota(jnp.int32, (768, 128), 1) < 16, small, 0).astype(bf16), cols)
    dl_high, dl_low = split(dlog)
    gs = lax.dot_general(n2, dl_high, (rows, ((), ())), preferred_element_type=f32)
    gs = gs + lax.dot_general(n2, dl_low, (rows, ((), ())), preferred_element_type=f32)
    b_high, b_low = split(lane_of(beta[0], 18) + lane_of(beta[1], 19))
    gs = gs + lax.dot_general(og_low, b_high, (rows, ((), ())), preferred_element_type=f32)
    gs_out[...] = gs + lax.dot_general(og_low, b_low, (rows, ((), ())), preferred_element_type=f32)
    mixed = lax.dot_general(prev[...], jnp.where(lane < 12, dlog, 0.0), (rows, ((), ())), preferred_element_type=f32,
                            precision=lax.Precision.HIGHEST)
    misc_out[0:16, :] = mixed[0:16]
    misc_out[16:24, :] = jnp.broadcast_to(jnp.sum(prob * live, axis=0, keepdims=True), (8, 128))
    sum_step(7)

    din = jnp.concatenate([s.total(0), s.total(1)], axis=0).astype(bf16)
    into = ((1,), (0,))
    d_out[...] = exact_dot(pg_far[:, 0:192], din, into).astype(bf16)
    swaps[2].start()
    dn_near = dn_near + exact_dot(pg_own[:, 0:192], din, into)
    swaps[2].wait_recv()
    dn = dn_near + d_in[...].astype(f32)
    t = dn * smt[17:18, :]
    rg = og + scale * (t - xh * (jnp.sum(t * xh, axis=1, keepdims=True) * (1.0 / 768)))
    res_out[...] = rg
    ag_out[...] = lax.dot_general(rg.astype(bf16), wout[...], (cols, ((), ())), preferred_element_type=f32).astype(bf16)
    gain = jnp.broadcast_to(jnp.sum(dn * xh, axis=0, keepdims=True), (128, 768))
    gs_out[...] += jnp.where(lax.broadcasted_iota(jnp.int32, (768, 128), 1) == 17, jnp.transpose(gain), 0.0)

    for n in early:
        outs.join_y(*n)
    for k in EARLY:
        part_store(k, False).start()
    g.finish()
    s.finish()
    outs.finish(EARLY, ())
    each(lambda k: gate_copy(k).wait_send())
    each(lambda k: vs_copy(k).wait_send())
    for c in swaps:
        c.wait_send()
    for k in range(4):
        part_store(k, k not in EARLY).wait()
    store_g(3, lambda c: c.wait())


def front_kernel(n_blk, *refs):
    (lengths, tok, cot, routes_t, w_in, router_t, const_t, gains_t, vec_t, wo_in, prev_t, mix_in, cos_hbm, sin_hbm, w_hbm,
     norm_hbm, q_hbm, k_hbm, v_hbm, o_hbm, part_hbm, g_hbm, att, smt, cnt, local_out, res_out, ag_out, gs_out, misc_out, pg_out,
     gain_out, sm, wout, pt, cot_rows, turn, w, w_part, wsem, *scratch) = refs
    all_here = greet_all(lax.axis_index("head"), lax.axis_index("blk"), n_blk)
    w_loads = [pltpu.make_async_copy(w_hbm.at[:, kind], w_part.at[kind], wsem.at[kind]) for kind in range(3)]
    for c in w_loads:
        c.start()
    turn[...] = jnp.zeros_like(turn)
    turn[0, 0:12, 0:24] = router_t[...].astype(f32)
    turn[0, 12:16, 0:24] = const_t[...].astype(f32)
    turn[0, 16:18, 0:24] = gains_t[...].astype(f32)
    turn[0, 18:20, 0:24] = vec_t[...].astype(f32)
    turn[1, 0:2, :] = routes_t[...].astype(f32)
    turn[2, 0:12, :] = prev_t[...]
    turn[3, 0:12, 0:12] = mix_in[...]
    small = jnp.transpose(turn[0])[0:24, 0:64]
    gain_out[...] = small
    routes = jnp.transpose(turn[1])
    prev = jnp.transpose(turn[2])

    def relay_w(kind):
        w_loads[kind].wait()
        t = w_part[kind].astype(f32)
        for e in range(4):
            w[3 * e + kind] = t[:, e, :].astype(bf16)

    cot_gather, finish = forward_kernel(
        n_blk, all_here, lengths, tok, cot, routes, w_in, small, wo_in, cos_hbm, sin_hbm, relay_w, norm_hbm, q_hbm, k_hbm, v_hbm, o_hbm,
        att, smt, cnt, sm, wout, pt, cot_rows, *scratch[: len(forward_scratch(n_blk))])
    expert_kernel(
        n_blk, cot_gather, lengths, att, tok, cot, prev, turn.at[3], routes, wout, sm, smt, cnt, pt, w, cot_rows,
        part_hbm, g_hbm, local_out, res_out, ag_out, gs_out, misc_out, pg_out, *scratch[len(forward_scratch(n_blk)) :])
    finish()


def forward_scratch(n_blk):
    V, DMA = pltpu.VMEM, pltpu.SemaphoreType.DMA
    return [
        V((3, 16, 128, 256), bf16), V((12, 16, 384), bf16), V((2 * n_blk, 16, 384), bf16), V((768, 256), f32),
        V((768, 256), bf16), V((2048, 128), f32), V((2048, 128), f32), V((2048, 768), bf16), V((2048, 64), bf16),
        V((2048, 64), bf16), V((2048, 128), bf16), V((2048, 128), f32), V((16, 64, 128), bf16), V((12, 64, 128), bf16),
        V((128, 128), bf16), V((128, 128), bf16), V((128, 768), bf16), V((n_blk, 1, 2, 16, 1152), bf16),
        DMA((3, 16)), DMA((3, 16)), DMA((2 * n_blk,)), DMA((2 * n_blk,)), DMA((16,)), DMA((12,)), DMA((11,)), DMA((3,)), DMA((3,)),
        *gather_sems(1), *gather_sems(2),
    ]


def expert_scratch(n_blk):
    V, DMA = pltpu.VMEM, pltpu.SemaphoreType.DMA
    return [
        V((n_blk, 2, 96, 768), bf16),
        V((n_blk, 2, 96, 128), f32), V((n_blk, 2, 96, 256), bf16), V((n_blk, 2, 96, 128), bf16),
        V((n_blk, 2, 96, 768), bf16), V((n_blk, 2, 96, 768), bf16), V((3, 128, 768), f32),
        V((n_blk, 8, 256), f32), V((n_blk, 8, 256), f32), V((n_blk, 8, 256), f32),
        V((128, 768), bf16), V((128, 768), bf16), V((128, 128), f32), V((128, 128), f32),
        V((128, 768), bf16), V((128, 768), bf16), V((128, 128), f32), V((128, 128), f32),
        DMA((n_blk,)), DMA((n_blk,)), DMA((n_blk,)), DMA((n_blk,)), DMA((4,)), DMA((4,)), DMA((7,)),
        *gather_sems(2), *scatter_scratch(2, 96, 768),
        V((4, 2, 2, 96, 768), bf16), V((4, 2, 96, 768), bf16), DMA((4, 2, 2)), DMA((4, 2, 2)), DMA((4, 2)), DMA((4, 2)),
    ]


def front(lengths, tokens, cotangent, routes, w_qkv, w_router, w_const, gains, vec, w_out, prev, mix, w, n_blk):
    cos, sin = rotary_tables(2048)
    vm = pl.BlockSpec(memory_space=pltpu.VMEM)
    hbm = pl.BlockSpec(memory_space=pl.ANY)
    sds = jax.ShapeDtypeStruct
    V = pltpu.VMEM
    return pl.pallas_call(
        functools.partial(front_kernel, n_blk),
        out_shape=(
            sds((2048, 768), bf16), sds((2048, 64), bf16), sds((2048, 64), bf16), sds((2048, 128), bf16),
            sds((2048, 128), f32), sds((n_blk, 2, 96, 768), bf16), sds((128, 3, 4, 768), f32),
            sds((128, 768), bf16), sds((32, 768), f32), sds((8, 128), f32), sds((128, 768), f32), sds((128, 768), f32),
            sds((128, 768), bf16), sds((768, 128), f32), sds((24, 128), f32), sds((2, 128, 256), f32),
            sds((24, 64), f32),
        ),
        in_specs=[pl.BlockSpec(memory_space=pltpu.SMEM)] + [vm] * 11 + [hbm] * 3,
        out_specs=(hbm,) * 7 + (vm,) * 10,
        scratch_shapes=[
            V((768, 128), bf16), V((768, 768), bf16), V((2, 128, 256), bf16), V((n_blk, 2, 96, 768), bf16),
            V((4, 128, 128), f32), V((12, 128, 768), bf16), V((3, 128, 4, 768), bf16), pltpu.SemaphoreType.DMA((3,)),
            *forward_scratch(n_blk), *expert_scratch(n_blk),
        ],
        compiler_params=pltpu.CompilerParams(collective_id=0, has_side_effects=True, vmem_limit_bytes=63 * 2**20),
        cost_estimate=pl.CostEstimate(flops=8 * 10**9, bytes_accessed=3 * 10**7, transcendentals=0),
        name="front",
    )(lengths, tokens, cotangent, routes.T, w_qkv, w_router.T, w_const.T, gains.T, vec.T, w_out, prev.T, mix,
      jnp.asarray(cos), jnp.asarray(sin), w)


def backward_kernel(
    n_blk, lengths, ag, tok, res_grad, smt, att, local_out, pg, g_small, misc, w_own, small, cnt,
    norm_hbm, q_hbm, k_hbm, v_hbm, o_hbm, cos_hbm, sin_hbm, w_hbm, part_hbm,
    out, dtok_out, gq_out, go_out, router_out, const_out, vec_out, gains_out, mix_out, aux_out,
    norm, q, k, v, o, cos, sin, w_all, agbuf, do_in, do, dk, dv, dqkv, obuf, got, dproj, turn, g_f, gbuf, g_in,
    part, gpart, gfar, gsum, far_out, far_in, misc_sum, misc_in,
    a_send, a_recv, b_send, b_recv, g_send, g_recv, loc, x_send, x_recv, m_send, m_recv, *rest,
):
    h, b = lax.axis_index("head"), lax.axis_index("blk")
    me = b * 2 + h
    total = 2 * n_blk
    _, _, rank = place(0, h, b)
    base = (b // 8) * 8
    head = head_of(h, b)
    working = (b % 4) != 3
    all_here = greet_all(h, b, n_blk)
    loads = [
        pltpu.make_async_copy(src, dst, loc.at[i])
        for i, (src, dst) in enumerate([
            (q_hbm, q), (k_hbm, k), (v_hbm, v), (o_hbm, o), (cos_hbm, cos), (sin_hbm, sin), (norm_hbm, norm),
            (w_hbm, w_all), (part_hbm, part)])
    ]
    for c in loads:
        c.start()
    a = ag[...].astype(f32)
    for j in range(12):
        agbuf[j] = jnp.concatenate([a[0:64, 64 * j : 64 * j + 64], a[64:128, 64 * j : 64 * j + 64]], axis=1).astype(bf16)
    all_here()

    def to_head(j):
        r = home_of(j)
        return pltpu.make_async_remote_copy(
            src_ref=agbuf.at[j], dst_ref=do_in.at[rank], send_sem=a_send.at[j], recv_sem=a_recv.at[rank],
            device_id=(r % 2, base + r // 2), device_id_type=MESH,
        )

    for j in range(12):
        @pl.when(rank != home_of(j))
        def _(j=j):
            to_head(j).start()

    def to_tokens(r):
        return pltpu.make_async_remote_copy(
            src_ref=obuf.at[r], dst_ref=got.at[head], send_sem=b_send.at[r], recv_sem=b_recv.at[head],
            device_id=(r % 2, base + r // 2), device_id_type=MESH,
        )

    def to_owner(kk):
        other = (me + kk) % total
        oh, ob = other % 2, other // 2
        return pltpu.make_async_remote_copy(
            src_ref=gbuf.at[oh * n_blk + ob], dst_ref=g_in.at[me], send_sem=g_send.at[kk], recv_sem=g_recv.at[me],
            device_id=(oh, ob), device_id_type=MESH,
        )

    length = lengths[b // 8]

    rs = RowScatter(part, *rest[0:3], rest[3:9], h, b)
    gs = RowScatter(gsum, *rest[9:12], rest[12:18], h, b)
    g_f2 = lax.dot_general(att[...], res_grad[...].astype(bf16), (((0,), (0,)), ((), ())), preferred_element_type=f32)
    for w in range(total):
        cat = jnp.concatenate([g_f2[24 * w : 24 * w + 24], g_small[24 * w : 24 * w + 24, :]], axis=1)
        gpart[w // n_blk, w % n_blk, 0] = fold(cat)
    swaps = [
        pltpu.make_async_remote_copy(
            src_ref=src, dst_ref=dst, send_sem=x_send.at[n], recv_sem=x_recv.at[n],
            device_id=(1 - h, b), device_id_type=MESH)
        for n, (src, dst) in enumerate([(gpart.at[1 - h], gfar), (far_out, far_in)])
    ]
    swaps[0].start()

    def join_planes():
        swaps[0].wait_recv()
        gsum[...] = (gpart[h].astype(f32) + gfar[...].astype(f32)).astype(bf16)
        for n in gs.order:
            gs.send_core(*n)

    loads[8].wait()
    late = [(k, p) for k in (3, 2, 1, 0) if k not in EARLY for p in range(2)]
    def z_early(ks):
        for kk in ks:
            if kk in EARLY and kk:
                for p in range(2):
                    rs.to_z(kk, p).start()

    z_early(Z_FIRST)
    for n in late:
        rs.send_core(*n)

    misc_sum[0] = misc[...]
    z = b // 4
    partners = [(1 - h, b), (h, b + 1 - 2 * (b % 2)), (h, b + 2 - 4 * ((b // 2) % 2)),
                (h, b + 4 - 8 * (z % 2)), (h, b + 8 - 16 * (z // 2))]

    def pairwise(t):
        return pltpu.make_async_remote_copy(
            src_ref=misc_sum.at[t], dst_ref=misc_in.at[t], send_sem=m_send.at[t], recv_sem=m_recv.at[t],
            device_id=partners[t], device_id_type=MESH)

    def pairwise_done(t):
        pairwise(t).wait_recv()
        misc_sum[t + 1] = misc_sum[t] + misc_in[t]
        if t < 4:
            pairwise(t + 1).start()

    pairwise(0).start()
    def step(scatter, stage, n):
        k, p = scatter.order[n]
        return lambda: getattr(scatter, stage)(k, p)

    def ry(n):
        return lambda: rs.send_y(*late[n]) if n < len(late) else None

    def rz(n):
        return lambda: rs.send_z(*late[n]) if n < len(late) else None

    def gy(n):
        return step(gs, "send_y", n)

    def gz(n):
        return step(gs, "send_z", n)

    def pd(t):
        return lambda: pairwise_done(t)

    between = {
        8: [ry(0), pd(0)], 7: [], 6: [], 5: [], 4: [ry(1), pd(1)], 3: [], 2: [], 1: [],
        0: [join_planes, ry(2), pd(2)],
    }

    @pl.when(jnp.logical_not(working))
    def _():
        do_in[...] = jnp.zeros_like(do_in)

    @pl.when(working)
    def _():
        do_in[rank] = agbuf[head]

    for c in loads[:6]:
        c.wait()
    if True:
        def unpack(r, carry):
            @pl.when((r != rank) & working)
            def _():
                pltpu.make_async_remote_copy(
                    src_ref=agbuf.at[0], dst_ref=do_in.at[r], send_sem=a_send.at[0], recv_sem=a_recv.at[r],
                    device_id=(h, b), device_id_type=MESH,
                ).wait_recv()

            t = do_in[r].astype(f32)
            rows = pl.multiple_of(r * 128, 128)
            do[pl.ds(rows, 64), :] = t[:, 0:64].astype(bf16)
            do[pl.ds(rows + 64, 64), :] = t[:, 64:128].astype(bf16)
            return carry

        lax.fori_loop(0, 16, unpack, 0)
        for act in between[8]:
            act()
        for i in range(7, -1, -1):
            width = 256 * (i + 1)
            lo = 256 * i
            qi, doi = q[lo:width, :], do[lo:width, :]
            s = lax.dot_general(qi, k[0:width, :], (((1,), (1,)), ((), ())), preferred_element_type=f32)
            key = lax.broadcasted_iota(jnp.int32, (1, width), 1)
            ov = o[lo:width, :]
            lse = ov[:, 64:65]
            s = (s - lse) + jnp.where(key < length, 0.0, NEG)
            rowi = lax.broadcasted_iota(jnp.int32, (256, 256), 0)
            coli = lax.broadcasted_iota(jnp.int32, (256, 256), 1)
            last = jnp.where(coli <= rowi, s[:, lo:], NEG)
            s = last if i == 0 else jnp.concatenate([s[:, :lo], last], axis=1)
            p = jnp.exp(s)
            dp = lax.dot_general(doi, v[0:width, 0:64], (((1,), (1,)), ((), ())), preferred_element_type=f32)
            inner = jnp.sum(doi.astype(f32) * ov[:, 0:64], axis=1, keepdims=True)
            ds = (p * (dp - inner)).astype(bf16)
            p = p.astype(bf16)
            dq = jnp.dot(ds, k[0:width, :], preferred_element_type=f32) * 0.125
            dki = lax.dot_general(ds, qi, (((0,), (0,)), ((), ())), preferred_element_type=f32)
            dvi = lax.dot_general(p, doi, (((0,), (0,)), ((), ())), preferred_element_type=f32)
            if i == 7:
                dk[...] = dki
                dv[...] = dvi
            else:
                dk[0:width, :] += dki
                dv[0:width, :] += dvi
            both = jnp.concatenate([dq, dk[lo:width, :]], axis=1)
            both = turned(both, cos[lo:width, :], -sin[lo:width, :]).astype(bf16)
            dvl = dv[lo:width, :]
            dqkv[lo:width, 0:128] = both
            dqkv[lo:width, 128:256] = jnp.concatenate([dvl, jnp.zeros_like(dvl)], axis=1).astype(bf16)
            for half in range(2):
                r = 2 * i + half
                obuf[r, 0:128, :] = both[128 * half : 128 * half + 128]
                obuf[r, 128:192, :] = jnp.concatenate(
                    [dvl[128 * half : 128 * half + 64], dvl[128 * half + 64 : 128 * half + 128]], axis=1).astype(bf16)

                @pl.when((r != rank) & working)
                def _(r=r):
                    to_tokens(r).start()
            for act in between[i]:
                act()

        @pl.when(working)
        def _():
            got[head] = obuf[rank]

        loads[6].wait()
        for c in range(3):
            g_f[256 * c : 256 * c + 256, :] = lax.dot_general(
                norm[:, 256 * c : 256 * c + 256], dqkv[...], (((0,), (0,)), ((), ())), preferred_element_type=f32)
        for w in range(total):
            gbuf[w] = fold(g_f[24 * w : 24 * w + 24, :])

        def send_g(kk, carry):
            to_owner(kk).start()
            return carry

        @pl.when(working)
        def _():
            lax.fori_loop(1, total, send_g, 0)
            g_in[me] = gbuf[h * n_blk + b]

    z_early([kk for kk in (3, 2, 1) if kk not in Z_FIRST])
    for act in (*(ry(n) for n in range(3, len(late))), gy(0), gy(1), gy(2), gy(3), rz(0)):
        act()
    rz(1)()
    pairwise_done(3)

    for j in range(12):
        @pl.when(rank != home_of(j))
        def _(j=j):
            pltpu.make_async_remote_copy(
                src_ref=obuf.at[0], dst_ref=got.at[j], send_sem=b_send.at[0], recv_sem=b_recv.at[j],
                device_id=(h, b), device_id_type=MESH,
            ).wait_recv()
    for j in range(0, 12, 2):
        one, two = got[j].astype(f32), got[j + 1].astype(f32)
        lo = 64 * j
        for part_i, at in enumerate((0, 64)):
            dproj[:, 768 * part_i + lo : 768 * part_i + lo + 128] = jnp.concatenate(
                [one[0:128, at : at + 64], two[0:128, at : at + 64]], axis=1).astype(bf16)
        dproj[0:64, 1536 + lo : 1664 + lo] = jnp.concatenate([one[128:192, 0:64], two[128:192, 0:64]], axis=1).astype(bf16)
        dproj[64:128, 1536 + lo : 1664 + lo] = jnp.concatenate([one[128:192, 64:128], two[128:192, 64:128]], axis=1).astype(bf16)
    loads[7].wait()
    dn = lax.dot_general(dproj[...], w_all[...], (((1,), (1,)), ((), ())), preferred_element_type=f32)
    pairwise_done(4)
    x = tok[...].astype(f32)
    scale = lax.rsqrt(jnp.sum(x * x, axis=1, keepdims=True) * (1.0 / 768) + 1e-6)
    xh = x * scale
    t = dn * smt[16:17, :]
    dx = scale * (t - xh * (jnp.sum(t * xh, axis=1, keepdims=True) * (1.0 / 768)))
    dtok_out[...] = (res_grad[...] + dx).astype(bf16)

    for n in range(2, len(late)):
        rz(n)()
    rows = jnp.concatenate([rs.total(0), rs.total(1)], axis=0).astype(bf16)
    far_out[...] = exact_dot(pg[1, :, 0:192], rows, ((1,), (0,))).astype(bf16)
    swaps[1].start()
    for n in range(4):
        gz(n)()
    own = exact_dot(pg[0, :, 0:192], rows, ((1,), (0,))) + local_out[...]

    for src in range(total):
        if (src // 2) % 4 == 3:
            continue

        @pl.when(me != src)
        def _(src=src):
            pltpu.make_async_remote_copy(
                src_ref=gbuf.at[0], dst_ref=g_in.at[src], send_sem=g_send.at[0], recv_sem=g_recv.at[src],
                device_id=(h, b), device_id_type=MESH,
            ).wait_recv()
    for j in range(0, 12, 2):
        pair = []
        for jj in (j, j + 1):
            t = sum(g_in[16 * s + home_of(jj)].astype(f32) for s in range(total // 16))
            pair.append(jnp.concatenate(
                [t[:, 0:256], jnp.concatenate([t[0:8, 256:384], t[8:16, 256:384]], axis=1)], axis=0))
        one, two = pair
        for part in range(3):
            gq_out[:, 768 * part + 64 * j : 768 * part + 64 * j + 128] = jnp.concatenate(
                [one[:, 64 * part : 64 * part + 64], two[:, 64 * part : 64 * part + 64]], axis=1)

    lane = lax.broadcasted_iota(jnp.int32, (24, 128), 1)
    gain_grad = jnp.sum(gq_out[...] * w_own[...].astype(f32), axis=1, keepdims=True) / small[:, 16:17]
    t = gs.total(0)
    t = jnp.concatenate([t[:, 0:896], jnp.concatenate([t[0:8, 896:1344], t[8:16, 896:1344]], axis=1)], axis=0)
    go_out[...] = t[:, 0:768]
    turn[...] = jnp.zeros_like(turn)
    turn[0:24, :] = jnp.where(lane == 16, gain_grad, t[:, 768:896])
    t = jnp.transpose(turn[...])
    router_out[...] = t[0:12, 0:24]
    const_out[...] = t[12:16, 0:24]
    gains_out[...] = t[16:18, 0:24]
    vec_out[...] = t[18:20, 0:24]
    t = misc_sum[5]
    mix_out[...] = t[0:12, 0:12]
    live_total = (lengths[0] + lengths[1]).astype(f32)
    aux = cnt[0:1, :] / (2.0 * live_total) * (t[16:17, :] / live_total)
    aux_out[...] = 12.0 * jnp.sum(aux, axis=1, keepdims=True)
    swaps[1].wait_recv()
    out[...] = (own + far_in[...].astype(f32)).astype(bf16)

    rs.finish([k for k in range(4) if k not in EARLY])
    gs.finish()
    for t in range(5):
        pairwise(t).wait_send()
    for c in swaps:
        c.wait_send()
    for j in range(12):
        @pl.when(rank != home_of(j))
        def _(j=j):
            to_head(j).wait_send()

    @pl.when(working)
    def _():
        for r in range(16):
            @pl.when(r != rank)
            def _(r=r):
                to_tokens(r).wait_send()

        def sent(kk, carry):
            to_owner(kk).wait_send()
            return carry

        lax.fori_loop(1, total, sent, 0)


def attend_back(
    lengths, ag, tok, res_grad, smt, att, local_out, pg, g_small, misc, w_own, small, cnt, norm, q, k, v, o, w_all, parts,
    n_blk,
):
    cos, sin = rotary_tables(2048)
    vm = pl.BlockSpec(memory_space=pltpu.VMEM)
    hbm = pl.BlockSpec(memory_space=pl.ANY)
    sds = jax.ShapeDtypeStruct
    DMA = pltpu.SemaphoreType.DMA
    V = pltpu.VMEM
    total = 2 * n_blk
    return pl.pallas_call(
        functools.partial(backward_kernel, n_blk),
        out_shape=(
            sds((128, 768), bf16), sds((128, 768), bf16), sds((24, 2304), f32), sds((24, 768), f32), sds((12, 24), f32),
            sds((4, 24), f32), sds((2, 24), f32), sds((2, 24), f32), sds((12, 12), f32), sds((1, 1), f32),
        ),
        in_specs=[pl.BlockSpec(memory_space=pltpu.SMEM)] + [vm] * 12 + [hbm] * 9,
        out_specs=(vm,) * 10,
        scratch_shapes=[
            V((2048, 768), bf16), V((2048, 64), bf16), V((2048, 64), bf16), V((2048, 128), bf16), V((2048, 128), f32),
            V((2048, 128), f32), V((2048, 128), f32), V((768, 2304), bf16),
            V((12, 64, 128), bf16), V((16, 64, 128), bf16), V((2048, 64), bf16), V((2048, 64), f32), V((2048, 64), f32),
            V((2048, 256), bf16), V((16, 192, 128), bf16), V((12, 192, 128), bf16), V((128, 2304), bf16), V((128, 128), f32),
            V((768, 256), f32), V((total, 16, 384), bf16), V((total, 16, 384), bf16),
            V((n_blk, 2, 96, 768), bf16), V((2, n_blk, 1, 16, 1344), bf16), V((n_blk, 1, 16, 1344), bf16), V((n_blk, 1, 16, 1344), bf16),
            V((128, 768), bf16), V((128, 768), bf16),
            V((6, 24, 128), f32), V((5, 24, 128), f32),
            DMA((12,)), DMA((16,)), DMA((16,)), DMA((12,)), DMA((total,)), DMA((total,)), DMA((9,)), DMA((2,)), DMA((2,)),
            DMA((5,)), DMA((5,)), *scatter_scratch(2, 96, 768), *scatter_scratch(1, 16, 1344),
        ],
        compiler_params=pltpu.CompilerParams(collective_id=1, has_side_effects=True, vmem_limit_bytes=60 * 2**20),
        cost_estimate=pl.CostEstimate(flops=2 * 10**9, bytes_accessed=2 * 10**7, transcendentals=0),
        name="attend_back",
    )(lengths, ag, tok, res_grad, smt, att, local_out, pg, g_small, misc, w_own, small, cnt, norm, q, k, v, o,
      jnp.asarray(cos), jnp.asarray(sin), w_all, parts)


CAP = 24


eps = 1e-06
aux_weight = 0.01
highest = lax.Precision.HIGHEST
masked_score = -1e30


def shifted(block, axis, distance):
    devices = range(lax.axis_size(axis))
    route = [(i - distance, i) for i in devices if i - distance in devices]
    return lax.ppermute(block, axis, route)


def for_sending(x):
    return jax.tree.map(lambda a: a.astype(jnp.bfloat16) if a.dtype == jnp.float32 else a, x)


def rms_norm(values, gain_vector):
    return values * lax.rsqrt(jnp.mean(values * values, axis=-1, keepdims=True) + eps) * gain_vector


def rotary(values, positions, turn_sign):
    half_width = values.shape[-1] // 2
    frequency = jnp.exp(
        jnp.arange(half_width, dtype=jnp.float32) * (-2.0 * math.log(10000.0) / values.shape[-1])
    )
    angles = positions.astype(jnp.float32)[:, None] * frequency[None, :]
    cosine = jnp.cos(angles)[:, None, :]
    sine_part = turn_sign * jnp.sin(angles)[:, None, :]
    first_half = values[..., :half_width]
    second_half = values[..., half_width:]
    return jnp.concatenate(
        [
            first_half * cosine - second_half * sine_part,
            second_half * cosine + first_half * sine_part,
        ],
        axis=-1,
    )


def slot_lengths(slot_ids, lengths):
    slot_table = jnp.arange(lengths.shape[0], dtype=jnp.int32)
    return jnp.sum(jnp.where(slot_ids[:, None] == slot_table[None, :], lengths[None, :], 0), axis=1)


def allowed_mask(query_ids, key_ids, slot_size, lengths):
    query_slot = query_ids // slot_size
    key_slot = key_ids // slot_size
    query_pos = query_ids - query_slot * slot_size
    key_pos = key_ids - key_slot * slot_size
    key_live = (key_pos < slot_lengths(key_slot, lengths)) & (key_ids >= 0)
    return (
        (query_slot[:, None] == key_slot[None, :])
        & (key_pos[None, :] <= query_pos[:, None])
        & key_live[None, :]
    )


def masked_scores(query_block, key_head, query_ids, key_ids, slot_size, lengths):
    scores = lax.dot_general(
        query_block, key_head, (((1,), (1,)), ((), ())), preferred_element_type=jnp.float32
    ) * HD ** (-0.5)
    return jnp.where(allowed_mask(query_ids, key_ids, slot_size, lengths), scores, masked_score)


def attend_forward(queries, key_all, value_all, query_ids, key_ids, slot_size, lengths):
    head_total = queries.shape[1] // HD

    def one_head(head_index):
        query_head = lax.dynamic_slice_in_dim(queries, head_index * HD, HD, 1)
        key_head = lax.dynamic_slice_in_dim(key_all, head_index * HD, HD, 1)
        value_head = lax.dynamic_slice_in_dim(value_all, head_index * HD, HD, 1)
        scores = masked_scores(query_head, key_head, query_ids, key_ids, slot_size, lengths)
        row_max = jnp.max(scores, axis=1, keepdims=True)
        weights = jnp.exp(scores - row_max)
        row_total = jnp.sum(weights, axis=1, keepdims=True)
        probs_low = (weights / row_total).astype(jnp.bfloat16)
        head_outputs = [jnp.dot(probs_low, value_head, preferred_element_type=jnp.float32)]
        log_parts = [row_max[:, 0] + jnp.log(row_total[:, 0])]
        return (jnp.concatenate(head_outputs, axis=0), jnp.concatenate(log_parts, axis=0))

    head_outputs, log_sums = lax.map(one_head, jnp.arange(head_total, dtype=jnp.int32))
    return (head_outputs.transpose(1, 0, 2).reshape(queries.shape[0], queries.shape[1]), log_sums)


def attend_backward(
    queries, key_all, value_all, out_grads, log_sums, query_ids, key_ids, slot_size, lengths
):
    head_total = queries.shape[1] // HD
    block_rows = min(512, queries.shape[0])

    def one_head(head_index):
        query_head = lax.dynamic_slice_in_dim(queries, head_index * HD, HD, 1)
        key_head = lax.dynamic_slice_in_dim(key_all, head_index * HD, HD, 1)
        value_head = lax.dynamic_slice_in_dim(value_all, head_index * HD, HD, 1)
        grad_head = lax.dynamic_slice_in_dim(out_grads, head_index * HD, HD, 1)
        log_head = lax.dynamic_index_in_dim(log_sums, head_index, 0, keepdims=False)
        key_grad = jnp.zeros(key_head.shape, jnp.float32)
        value_grad = jnp.zeros(value_head.shape, jnp.float32)
        grad_block = grad_head[0:block_rows]
        scores = masked_scores(query_head, key_head, query_ids, key_ids, slot_size, lengths)
        probs = jnp.exp(scores - log_head[0:block_rows][:, None])
        probs_low = probs.astype(jnp.bfloat16)
        prob_grads = lax.dot_general(
            grad_block, value_head, (((1,), (1,)), ((), ())), preferred_element_type=jnp.float32
        )
        row_inner = jnp.sum(probs * prob_grads, axis=1, keepdims=True)
        score_grads = (probs * (prob_grads - row_inner)).astype(jnp.bfloat16)
        query_parts = [
            jnp.dot(score_grads, key_head, preferred_element_type=jnp.float32) * HD ** (-0.5)
        ]
        key_grad = key_grad + lax.dot_general(
            score_grads, query_head, (((0,), (0,)), ((), ())), preferred_element_type=jnp.float32
        ) * HD ** (-0.5)
        value_grad = value_grad + lax.dot_general(
            probs_low, grad_block, (((0,), (0,)), ((), ())), preferred_element_type=jnp.float32
        )
        return (jnp.concatenate(query_parts, axis=0), key_grad, value_grad)

    query_grad, key_grad, value_grad = lax.map(one_head, jnp.arange(head_total, dtype=jnp.int32))
    return (
        query_grad.transpose(1, 0, 2).reshape(queries.shape[0], queries.shape[1]),
        key_grad.transpose(1, 0, 2).reshape(key_all.shape[0], key_all.shape[1]),
        value_grad.transpose(1, 0, 2).reshape(value_all.shape[0], value_all.shape[1]),
    )


def fetch_prev(key_heads, value_heads, span_count):
    key_parts = [key_heads]
    value_parts = [value_heads]
    for offset in range(1, span_count):
        arrived = shifted((key_heads, value_heads), "blk", offset)
        key_parts.append(arrived[0])
        value_parts.append(arrived[1])
    return (jnp.concatenate(key_parts, axis=0), jnp.concatenate(value_parts, axis=0))


def router_probs(normed, router_w, mixing, prev_scores):
    logits = jnp.dot(normed, router_w, precision=highest) + jnp.dot(
        prev_scores, mixing, precision=highest
    )
    return jax.nn.softmax(logits, axis=-1)


def branch_sum(router_prob, normed, const_w, vector_w, outputs_pair, choose, live_rows, real_count):
    gate_values = jnp.sum(choose * router_prob[:, None, :], axis=-1)
    expert_share = jnp.sum(choose * gate_values[:, :, None], axis=1) * live_rows[:, None]
    routed = jnp.sum(gate_values[:, :, None] * outputs_pair, axis=1)
    routed = routed + expert_share[:, real_count + 1 : real_count + 2] * normed
    const_count = vector_w.shape[1]
    const_mix = jax.nn.softmax(
        jnp.dot(normed, const_w, precision=highest).reshape(normed.shape[0], const_count, 2),
        axis=-1,
    )
    for const_index in range(const_count):
        const_out = (
            const_mix[:, const_index, 0:1] * normed
            + const_mix[:, const_index, 1:2] * vector_w[:, const_index][None, :]
        )
        routed = (
            routed
            + expert_share[:, real_count + 2 + const_index : real_count + 3 + const_index]
            * const_out
        )
    return routed


def on_device(
    tokens,
    cotangent,
    prev_logits,
    routes,
    lengths,
    w_qkv,
    w_out,
    w_router,
    w_const,
    const_vec,
    norm_gains,
    gate_mix,
    expert_weights,
):
    tok_dev = tokens.shape[0]
    model_width = tokens.shape[1]
    head_count = lax.axis_size("head")
    blk_count = lax.axis_size("blk")
    span_count = max(8, min(blk_count // 4, 8192 // (head_count * tok_dev)) * min(1, tok_dev // 64))
    head_index = lax.axis_index("head")
    blk_index = lax.axis_index("blk")
    slot_size = span_count * head_count * tok_dev
    tok_blk = head_count * tok_dev
    qkv_w, out_w, router_w, const_w, vector_w, gain_pair = (
        lax.all_gather(w_qkv, ("head", "blk"), axis=0, tiled=True),
        lax.all_gather(w_out, ("head", "blk"), axis=0, tiled=True),
        lax.all_gather(w_router, ("head", "blk"), axis=0, tiled=True),
        lax.all_gather(w_const, ("head", "blk"), axis=0, tiled=True),
        lax.all_gather(const_vec, ("head", "blk"), axis=0, tiled=True),
        lax.all_gather(norm_gains, ("head", "blk"), axis=0, tiled=True),
    )
    gain_pair = gain_pair.astype(jnp.float32)
    row_ids = (blk_index * head_count + head_index) * tok_dev + jnp.arange(tok_dev, dtype=jnp.int32)
    slot_ids = row_ids // slot_size
    positions = row_ids - slot_ids * slot_size
    live_rows = (positions < slot_lengths(slot_ids, lengths)).astype(jnp.float32)
    inputs = tokens.astype(jnp.float32)
    normed_one, norm_one_back = jax.vjp(rms_norm, inputs, gain_pair[:, 0])
    normed_one_low = normed_one.astype(jnp.bfloat16)
    projected = jnp.dot(normed_one_low, qkv_w, preferred_element_type=jnp.float32).reshape(
        tok_dev, 3, HEADS, HD
    )
    query_send = (
        rotary(projected[:, 0], positions, 1.0).astype(jnp.bfloat16).reshape(tok_dev, model_width)
    )
    key_send = (
        rotary(projected[:, 1], positions, 1.0).astype(jnp.bfloat16).reshape(tok_dev, model_width)
    )
    value_send = projected[:, 2].astype(jnp.bfloat16).reshape(tok_dev, model_width)
    query_heads, key_heads, value_heads = (
        lax.all_to_all(query_send, "head", split_axis=1, concat_axis=0, tiled=True),
        lax.all_to_all(key_send, "head", split_axis=1, concat_axis=0, tiled=True),
        lax.all_to_all(value_send, "head", split_axis=1, concat_axis=0, tiled=True),
    )
    blk_rows = blk_index * tok_blk + jnp.arange(tok_blk, dtype=jnp.int32)
    blk_pos = blk_rows - blk_rows // slot_size * slot_size
    key_ids = jnp.concatenate([blk_rows - offset * tok_blk for offset in range(span_count)], axis=0)
    key_all, value_all = fetch_prev(key_heads, value_heads, span_count)
    attended, log_sums = attend_forward(
        query_heads, key_all, value_all, blk_rows, key_ids, slot_size, lengths
    )
    attended_tok = lax.all_to_all(
        attended.astype(jnp.bfloat16), "head", split_axis=0, concat_axis=1, tiled=True
    )
    residual = inputs + jnp.dot(attended_tok, out_w, preferred_element_type=jnp.float32)
    normed_two, norm_two_back = jax.vjp(rms_norm, residual, gain_pair[:, 1])
    normed_two_low = normed_two.astype(jnp.bfloat16)
    normed_two_f = normed_two_low.astype(jnp.float32)
    router_prob, router_back = jax.vjp(
        partial(router_probs, prev_scores=prev_logits),
        normed_two_f,
        router_w.astype(jnp.float32),
        gate_mix,
    )
    expert_count = router_w.shape[1]
    real_count = expert_weights.shape[1] * head_count
    choose = (
        routes[:, :, None] == jnp.arange(expert_count, dtype=jnp.int32)[None, None, :]
    ).astype(jnp.float32)
    count_local = jnp.sum(jnp.sum(choose, axis=1) * live_rows[:, None], axis=0)
    prob_local = jnp.sum(router_prob * live_rows[:, None], axis=0)
    count_all, prob_all = lax.psum((count_local, prob_local), ("head", "blk"))
    live_total = jnp.sum(lengths).astype(jnp.float32)
    fraction = count_all / (2.0 * live_total)
    aux_loss = expert_count * jnp.sum(fraction * (prob_all / live_total))
    gate_values = jnp.sum(choose * router_prob[:, None, :], axis=-1)
    out_grad = live_rows[:, None] * cotangent.astype(jnp.float32)
    assigned = routes.reshape(-1)
    live_pairs = jnp.repeat(live_rows, 2)
    is_real = (assigned < real_count) & (live_pairs > 0)
    onehot = (
        (assigned[:, None] == jnp.arange(real_count, dtype=jnp.int32)[None, :]) & is_real[:, None]
    ).astype(jnp.int32)
    slot_rank = jnp.sum((jnp.cumsum(onehot, axis=0) - onehot) * onehot, axis=1)
    target = jnp.where(is_real, assigned * CAP + slot_rank, real_count * CAP)
    source = (
        jnp.full((real_count * CAP + 1,), 2 * tok_dev, jnp.int32)
        .at[target]
        .set(jnp.arange(2 * tok_dev, dtype=jnp.int32))[: real_count * CAP]
    )
    zero_row = jnp.zeros((1, model_width), jnp.bfloat16)
    send_rows = jnp.concatenate([normed_two_low, zero_row], axis=0)[source // 2].reshape(
        real_count, CAP, model_width
    )
    pair_grads = (gate_values.reshape(-1, 1) * jnp.repeat(out_grad, 2, axis=0)).astype(jnp.bfloat16)
    send_grads = jnp.concatenate([pair_grads, zero_row], axis=0)[source].reshape(
        real_count, CAP, model_width
    )
    expert_in, expert_cot = (
        lax.all_to_all(send_rows, "head", split_axis=0, concat_axis=1, tiled=True),
        lax.all_to_all(send_grads, "head", split_axis=0, concat_axis=1, tiled=True),
    )
    weight_piece = lax.all_gather(expert_weights, "blk", axis=0, tiled=True)
    gate_w = weight_piece[:, :, 0, :]
    up_w = weight_piece[:, :, 1, :]
    down_w = weight_piece[:, :, 2, :]
    gate_part = jnp.einsum("esd,ned->esn", expert_in, gate_w, preferred_element_type=jnp.float32)
    up_part = jnp.einsum("esd,ned->esn", expert_in, up_w, preferred_element_type=jnp.float32)
    sigmoid_part = jax.nn.sigmoid(gate_part)
    silu_part = gate_part * sigmoid_part
    hidden = (silu_part * up_part).astype(jnp.bfloat16)
    out_sum = jnp.einsum("esn,ned->esd", hidden, down_w, preferred_element_type=jnp.float32)
    hidden_grad = jnp.einsum("esd,ned->esn", expert_cot, down_w, preferred_element_type=jnp.float32)
    gate_grad = (
        hidden_grad * up_part * (sigmoid_part * (1.0 + gate_part * (1.0 - sigmoid_part)))
    ).astype(jnp.bfloat16)
    up_grad = (hidden_grad * silu_part).astype(jnp.bfloat16)
    in_grad = jnp.einsum("esn,ned->esd", gate_grad, gate_w, preferred_element_type=jnp.float32)
    in_grad = in_grad + jnp.einsum(
        "esn,ned->esd", up_grad, up_w, preferred_element_type=jnp.float32
    )
    hidden_all = hidden
    gate_all = gate_grad
    up_all = up_grad
    out_sum, in_grad, hidden_all, gate_all, up_all = (
        out_sum,
        in_grad,
        hidden_all,
        gate_all,
        up_all,
    )
    hidden_own, gate_own, up_own = (
        lax.all_to_all(hidden_all, "blk", split_axis=2, concat_axis=1, tiled=True),
        lax.all_to_all(gate_all, "blk", split_axis=2, concat_axis=1, tiled=True),
        lax.all_to_all(up_all, "blk", split_axis=2, concat_axis=1, tiled=True),
    )
    rows_in = lax.all_gather(expert_in, "blk", axis=1, tiled=True)
    rows_cot = lax.all_gather(expert_cot, "blk", axis=1, tiled=True)
    gate_w_grad = jnp.einsum("esn,esd->ned", gate_own, rows_in, preferred_element_type=jnp.float32)
    up_w_grad = jnp.einsum("esn,esd->ned", up_own, rows_in, preferred_element_type=jnp.float32)
    down_w_grad = jnp.einsum(
        "esn,esd->ned", hidden_own, rows_cot, preferred_element_type=jnp.float32
    )
    expert_grads = jnp.stack([gate_w_grad, up_w_grad, down_w_grad], axis=2)
    returned, returned_grad = (
        lax.all_to_all(
            out_sum.astype(jnp.bfloat16), "head", split_axis=1, concat_axis=0, tiled=True
        ),
        lax.all_to_all(
            in_grad.astype(jnp.bfloat16), "head", split_axis=1, concat_axis=0, tiled=True
        ),
    )
    outputs_pair = (
        jnp.concatenate([returned.reshape(-1, model_width), zero_row], axis=0)[target]
        .astype(jnp.float32)
        .reshape(tok_dev, 2, model_width)
    )
    input_pair = (
        jnp.concatenate([returned_grad.reshape(-1, model_width), zero_row], axis=0)[target]
        .astype(jnp.float32)
        .reshape(tok_dev, 2, model_width)
    )
    expert_input_grad = input_pair[:, 0] + input_pair[:, 1]
    branch, branch_back = jax.vjp(
        partial(branch_sum, choose=choose, live_rows=live_rows, real_count=real_count),
        router_prob,
        normed_two_f,
        const_w.astype(jnp.float32),
        vector_w.astype(jnp.float32),
        outputs_pair,
    )
    output = ((residual + branch) * live_rows[:, None]).astype(jnp.bfloat16)
    prob_grad, normed_grad_branch, const_grad, vector_grad, unused_grad = branch_back(out_grad)
    aux_grad = aux_weight * expert_count / live_total * fraction[None, :] * live_rows[:, None]
    normed_grad_router, router_grad, mixing_grad = router_back(prob_grad + aux_grad)
    normed_grad = normed_grad_router + normed_grad_branch + expert_input_grad
    residual_grad_norm, gain_two_grad = norm_two_back(normed_grad)
    residual_grad = out_grad + residual_grad_norm
    out_w_grad = jnp.dot(attended_tok.astype(jnp.float32).T, residual_grad, precision=highest)
    attended_grad = jnp.dot(residual_grad, out_w.astype(jnp.float32).T, precision=highest).astype(
        jnp.bfloat16
    )
    attended_grad_heads = lax.all_to_all(
        attended_grad, "head", split_axis=1, concat_axis=0, tiled=True
    )
    key_again, value_again = fetch_prev(key_heads, value_heads, span_count)
    query_grad, key_grad, value_grad = attend_backward(
        query_heads,
        key_again,
        value_again,
        attended_grad_heads,
        log_sums,
        blk_rows,
        key_ids,
        slot_size,
        lengths,
    )
    own_key = key_grad[:tok_blk]
    own_value = value_grad[:tok_blk]
    for offset in range(1, span_count):
        back_key, back_value = shifted(
            (
                for_sending(key_grad[offset * tok_blk : (offset + 1) * tok_blk]),
                for_sending(value_grad[offset * tok_blk : (offset + 1) * tok_blk]),
            ),
            "blk",
            -offset,
        )
        own_key = own_key + back_key
        own_value = own_value + back_value
    local_heads = query_heads.shape[1] // HD
    query_back = (
        rotary(query_grad.reshape(tok_blk, local_heads, HD), blk_pos, -1.0)
        .astype(jnp.bfloat16)
        .reshape(tok_blk, local_heads * HD)
    )
    key_back = (
        rotary(own_key.reshape(tok_blk, local_heads, HD), blk_pos, -1.0)
        .astype(jnp.bfloat16)
        .reshape(tok_blk, local_heads * HD)
    )
    value_back = own_value.astype(jnp.bfloat16)
    query_tok, key_tok, value_tok = (
        lax.all_to_all(query_back, "head", split_axis=0, concat_axis=1, tiled=True),
        lax.all_to_all(key_back, "head", split_axis=0, concat_axis=1, tiled=True),
        lax.all_to_all(value_back, "head", split_axis=0, concat_axis=1, tiled=True),
    )
    projected_grad = jnp.concatenate([query_tok, key_tok, value_tok], axis=1)
    qkv_grad = jnp.dot(normed_one_low.T, projected_grad, preferred_element_type=jnp.float32)
    normed_one_grad = jnp.dot(projected_grad, qkv_w.T, preferred_element_type=jnp.float32)
    inputs_grad_norm, gain_one_grad = norm_one_back(normed_one_grad)
    token_grad = (residual_grad + inputs_grad_norm).astype(jnp.bfloat16)
    weight_grads = (
        lax.psum_scatter(qkv_grad, ("head", "blk"), scatter_dimension=0, tiled=True),
        lax.psum_scatter(out_w_grad, ("head", "blk"), scatter_dimension=0, tiled=True),
        lax.psum_scatter(router_grad, ("head", "blk"), scatter_dimension=0, tiled=True),
        lax.psum_scatter(const_grad, ("head", "blk"), scatter_dimension=0, tiled=True),
        lax.psum_scatter(vector_grad, ("head", "blk"), scatter_dimension=0, tiled=True),
        lax.psum_scatter(
            jnp.stack([gain_one_grad, gain_two_grad], axis=1),
            ("head", "blk"),
            scatter_dimension=0,
            tiled=True,
        ),
    )
    mixing_total = lax.psum(mixing_grad, ("head", "blk"))
    return (
        output,
        aux_loss,
        token_grad,
        weight_grads[0],
        weight_grads[1],
        weight_grads[2],
        weight_grads[3],
        weight_grads[4],
        weight_grads[5],
        mixing_total,
        expert_grads,
    )


def settle_kernel(n, *refs):
    sources, results, (sems, *rooms) = refs[:n], refs[n : 2 * n], refs[2 * n :]
    ins, outs = [], []
    for i in range(n):
        parts = [(sources[i], rooms[i], results[i])]
        if i == n - 1:
            parts = [tuple(r.at[pl.ds(32 * c, 32)] for r in parts[0]) for c in range(4)]
        for src, room, dst in parts:
            ins.append(pltpu.make_async_copy(src, room, sems.at[0, len(ins)]))
            outs.append(pltpu.make_async_copy(room, dst, sems.at[1, len(outs)]))
    for c in ins[::-1]:
        c.start()
    for c, d in zip(ins[::-1], outs[::-1]):
        c.wait()
        d.start()
    for d in outs:
        d.wait()


def settle(*arrays):
    hbm = pl.BlockSpec(memory_space=pl.ANY)
    n = len(arrays)
    return pl.pallas_call(
        functools.partial(settle_kernel, n),
        out_shape=tuple(jax.ShapeDtypeStruct(a.shape, a.dtype) for a in arrays),
        in_specs=[hbm] * n,
        out_specs=(hbm,) * n,
        scratch_shapes=[pltpu.SemaphoreType.DMA((2, n + 3))] + [pltpu.VMEM(a.shape, a.dtype) for a in arrays],
        compiler_params=pltpu.CompilerParams(vmem_limit_bytes=63 * 2**20),
        name="settle",
    )(*arrays)


def on_device_small(
    tokens, cotangent, prev_logits, routes, lengths, w_qkv, w_out, w_router, w_const, const_vec, norm_gains, gate_mix,
    expert_weights,
):
    n_blk = lax.axis_size("blk")
    w_all = lax.all_gather(w_qkv, ("head", "blk"), axis=0, tiled=True)
    norm, q, k, v, o, parts, g_exp, att, smt, cnt, local_out, res_grad, att_grad, g_small, misc, pg, small = front(
        lengths, tokens, cotangent, routes, w_qkv, w_router, w_const, norm_gains, const_vec, w_out, prev_logits, gate_mix,
        expert_weights.transpose(0, 2, 1, 3), n_blk)
    output, token_grad, qkv_grad, g_out, g_router, g_const, g_vec, g_gains, g_mix, aux = attend_back(
        lengths, att_grad, tokens, res_grad, smt, att, local_out, pg, g_small, misc, w_qkv, small, cnt, norm, q, k, v, o, w_all,
        parts, n_blk)
    results = settle(output, token_grad, qkv_grad, g_out, g_router, g_const, g_vec, g_gains, g_mix, aux, g_exp)
    output, token_grad, qkv_grad, g_out, g_router, g_const, g_vec, g_gains, g_mix, aux, g_exp = results
    return (
        output, aux.reshape(()), token_grad, qkv_grad, g_out, g_router.T, g_const.T, g_vec.T, g_gains.T, g_mix,
        g_exp.transpose(0, 2, 1, 3),
    )


def solution(mesh):
    small = mesh.shape["blk"] == 16 and mesh.shape["head"] == 2
    return jax.shard_map(
        on_device_small if small else on_device,
        mesh=mesh,
        in_specs=(
            P(("blk", "head"), None),
            P(("blk", "head"), None),
            P(("blk", "head"), None),
            P(("blk", "head"), None),
            P(),
            P(("head", "blk"), None),
            P(("head", "blk"), None),
            P(("head", "blk"), None),
            P(("head", "blk"), None),
            P(("head", "blk"), None),
            P(("head", "blk"), None),
            P(),
            P("blk", "head", None, None),
        ),
        out_specs=(
            P(("blk", "head"), None),
            P(),
            P(("blk", "head"), None),
            P(("head", "blk"), None),
            P(("head", "blk"), None),
            P(("head", "blk"), None),
            P(("head", "blk"), None),
            P(("head", "blk"), None),
            P(("head", "blk"), None),
            P(),
            P("blk", "head", None, None),
        ),
        check_vma=False,
    )
```

profile of v0, /device:TPU:0, one launch (start us, length us, event | category | flops | bytes accessed | tf_op | source)
XLA Modules:
  0.0 258.9 jit_solution(3356801377252186050)
XLA Ops:
  7.2 0.0 all-gather.2.cloned.1.call-start
  7.2 0.7 all-gather.2.cloned.1.call-update
  7.9 177.7 %front.1 = (bf16[2048,768]{1,0:T(8,128)(2,1)}, bf16[2048,64]{1,0:T(8,128)(2,1)}, bf16[2048,64]{1,0:T(8,128)(2,1)}, bf16[2048,128]{1,0:T(8,128)(2,1)}, f32[2048,1...) custom-call(s32[2]{0:T(128)} %lengths.1, ...), custom_call_target="tpu_custom_call" | custom-call | flops 8000000000 | bytes 30000000 | tf_op jit(solution)/shard_map/front/pallas_call | solution.py:987
  185.7 0.0 all-gather.2.cloned.1.call-done.w_hbm
  185.7 61.1 %attend_back.1 = (bf16[128,768]{1,0:T(8,128)(2,1)}, bf16[128,768]{1,0:T(8,128)(2,1)}, f32[24,2304]{1,0:T(8,128)}, f32[24,768]{1,0:T(8,128)}, f32[12,24]{1,0:T(8,...) custom-call(s32[2]{0:T(128)} %lengths.1, ...), custom_call_target="tpu_custom_call" | custom-call | flops 2000000000 | bytes 20000000 | tf_op jit(solution)/shard_map/attend_back/pallas_call | solution.py:1349
  246.8 5.0 %settle.1 = (bf16[128,768]{1,0:T(8,128)(2,1)}, bf16[128,768]{1,0:T(8,128)(2,1)}, f32[24,2304]{1,0:T(8,128)}, f32[24,768]{1,0:T(8,128)}, f32[12,24]{1,0:T(8,128)}...) custom-call(bf16[128,768]{1,0:T(8,128)(2,1)} %get-tuple-element.65.r, ...), custom_call_target="tpu_custom_call" | custom-call | tf_op jit(solution)/shard_map/settle/pallas_call | solution.py:1839
Async XLA Ops:
  7.2 178.5 %all-gather.2.cloned.1.call-start = ((), (), s32[]{:S(2)}) async-start(), calls=%async_computation | async-start | bytes 3649536 | tf_op jit(solution)/shard_map/all_gather | solution.py:1855
Sparse Core Ops, SparseCore 0:
  10.9 73.3 all-gather.1
where the time goes:
time: 262 us; the launch traced here: 259 us
  Pallas kernels  244 us (93%)
  between operations  14.3 us (5%)
    pallas_call x1, Pallas kernels, front(): pl.pallas_call(functools.partial(front_kernel, n_blk), out_shape=(sds((20...  178 us
    pallas_call x1, Pallas kernels, attend_back(): pl.pallas_call(functools.partial(backward_kernel, n_blk), out_shape=(sds(...  61.1 us
  transfers between devices with their start and end apart: 1, of which 0 were waited for; matrix products, arithmetic and copies ran while one was open for 0% of the time, Pallas kernels for 69%

commit v1 on v0

--- a/solution.py
+++ b/solution.py
@@ -1029,7 +1029,7 @@
             (q_hbm, q), (k_hbm, k), (v_hbm, v), (o_hbm, o), (cos_hbm, cos), (sin_hbm, sin), (norm_hbm, norm),
             (w_hbm, w_all), (part_hbm, part)])
     ]
-    for c in loads:
+    for c in loads[8:] + loads[:8]:
         c.start()
     a = ag[...].astype(f32)
     for j in range(12):

time: 262 us -> 262 us (level)
  no operation moved by 1% of the time
where the time goes in v1:
time: 262 us; the launch traced here: 259 us
  Pallas kernels  244 us (93%)
  between operations  14.3 us (5%)
    pallas_call x1, Pallas kernels, front(): pl.pallas_call(functools.partial(front_kernel, n_blk), out_shape=(sds((20...  178 us
    pallas_call x1, Pallas kernels, attend_back(): pl.pallas_call(functools.partial(backward_kernel, n_blk), out_shape=(sds(...  61.1 us
  transfers between devices with their start and end apart: 1, of which 0 were waited for; matrix products, arithmetic and copies ran while one was open for 0% of the time, Pallas kernels for 69%

profile of v1, /device:TPU:0, one launch (start us, length us, event | category | flops | bytes accessed | tf_op | source)
XLA Modules:
  0.0 258.9 jit_solution(14579868409048317900)
XLA Ops:
  7.2 0.0 all-gather.2.cloned.1.call-start
  7.2 0.7 all-gather.2.cloned.1.call-update
  7.9 177.7 %front.1 = (bf16[2048,768]{1,0:T(8,128)(2,1)}, bf16[2048,64]{1,0:T(8,128)(2,1)}, bf16[2048,64]{1,0:T(8,128)(2,1)}, bf16[2048,128]{1,0:T(8,128)(2,1)}, f32[2048,1...) custom-call(s32[2]{0:T(128)} %lengths.1, ...), custom_call_target="tpu_custom_call" | custom-call | flops 8000000000 | bytes 30000000 | tf_op jit(solution)/shard_map/front/pallas_call | solution.py:987
  185.7 0.0 all-gather.2.cloned.1.call-done.w_hbm
  185.7 61.1 %attend_back.1 = (bf16[128,768]{1,0:T(8,128)(2,1)}, bf16[128,768]{1,0:T(8,128)(2,1)}, f32[24,2304]{1,0:T(8,128)}, f32[24,768]{1,0:T(8,128)}, f32[12,24]{1,0:T(8,...) custom-call(s32[2]{0:T(128)} %lengths.1, ...), custom_call_target="tpu_custom_call" | custom-call | flops 2000000000 | bytes 20000000 | tf_op jit(solution)/shard_map/attend_back/pallas_call | solution.py:1349
  246.8 5.0 %settle.1 = (bf16[128,768]{1,0:T(8,128)(2,1)}, bf16[128,768]{1,0:T(8,128)(2,1)}, f32[24,2304]{1,0:T(8,128)}, f32[24,768]{1,0:T(8,128)}, f32[12,24]{1,0:T(8,128)}...) custom-call(bf16[128,768]{1,0:T(8,128)(2,1)} %get-tuple-element.65.r, ...), custom_call_target="tpu_custom_call" | custom-call | tf_op jit(solution)/shard_map/settle/pallas_call | solution.py:1839
Async XLA Ops:
  7.2 178.5 %all-gather.2.cloned.1.call-start = ((), (), s32[]{:S(2)}) async-start(), calls=%async_computation | async-start | bytes 3649536 | tf_op jit(solution)/shard_map/all_gather | solution.py:1855
Sparse Core Ops, SparseCore 0:
  10.9 73.3 all-gather.1
